TPU v7x, 768 devices: a whole 4x8x12 slice. The times are simulated.
768 devices in a mesh: grp: 12 (over z), sub: 64 (over y, x, core).
Axes of the slice: x: 4, y: 8, z: 12, core: 2. Of those that a mesh axis runs over, the one named last changes fastest.
Arguments:
- users: bfloat16 [12288, 512], P(('grp', 'sub')), may hold values from -6 to 6
- node_ids: int32 [12288, 14], P(('grp', 'sub')), may hold values from 0 to 65535, as said below
- node_table: bfloat16 [65536, 128], P('sub'), may hold values from -6 to 6
- w_in: bfloat16 [640, 2048], replicated, may hold values from -0.25 to 0.25
- b_in: float32 [2048], replicated, may hold values from -3 to 3
- w_out: float32 [2048], replicated, may hold values from -3.6 to 3.6
- logit_grad: float32 [12288, 14], P(('grp', 'sub')), may hold values from -6 to 6
Outputs:
- user_grad: float32 [12288, 512], P(('grp', 'sub'))
- node_grad: float32 [65536, 128], P('sub')
- w1_grad: float32 [2048, 640], P('sub')
Inputs may be any that keep to these rules, and one draw needn't show every extreme that they name: `node_ids`: every id lies in 0 to 65535; the shard of id n is n // 1024. Among the 224 pairs of the rows of one device (aligned blocks of 16 rows), at most 7 lie on one shard, and in every block some shard has exactly 7; one shard has exactly 7 in every block.
All inputs are finite; a program needn't handle non-finite values.
Results may differ from a plain program's by a relative error of at most 0.02.
Values may be sent and summed in bfloat16 or wider, within the bound.
A program may use at most 32 MiB of HBM per device.

v0:
```python
import jax
import jax.numpy as jnp
from jax import lax
from jax.sharding import PartitionSpec as P


def grad_pass(inputs, upstream, w_in, b_in, w_out):
    pre_act = jnp.dot(inputs, w_in, preferred_element_type=jnp.float32) + b_in
    squash = jax.nn.sigmoid(pre_act)
    pre_grad = (upstream[:, None] * w_out * squash * (1.0 + pre_act * (1.0 - squash))).astype(
        jnp.bfloat16
    )
    in_grad = lax.dot_general(
        pre_grad, w_in, (((1,), (1,)), ((), ())), preferred_element_type=jnp.float32
    ).astype(jnp.bfloat16)
    return (pre_grad, in_grad)


def node_lookup(wanted, node_table):
    select = (wanted[:, None] == jnp.arange(node_table.shape[0])[None, :]).astype(jnp.bfloat16)
    fetched = jnp.dot(select, node_table, preferred_element_type=jnp.float32).astype(jnp.bfloat16)
    return (select, fetched)


def lead_product(left, right):
    return lax.dot_general(
        left, right, (((0,), (0,)), ((), ())), preferred_element_type=jnp.float32
    )


def local(users, node_ids, node_table, w_in, b_in, w_out, logit_grad):
    n_sub = lax.axis_size("sub")
    n_grp = lax.axis_size("grp")
    row_count, per_row = node_ids.shape
    user_width = users.shape[1]
    table_rows = node_table.shape[0]
    pair_count = row_count * per_row
    capacity = (2 * pair_count + n_sub - 1) // n_sub
    slot_tally_count = n_sub * capacity
    flat_ids = node_ids.reshape(-1)
    owner_of = flat_ids // table_rows
    local_of = flat_ids % table_rows
    owner_hit = (owner_of[:, None] == jnp.arange(n_sub)[None, :]).astype(jnp.int32)
    before = jnp.sum((jnp.cumsum(owner_hit, axis=0) - owner_hit) * owner_hit, axis=1)
    slot_of = owner_of * capacity + before
    placed = slot_of[:, None] == jnp.arange(slot_tally_count)[None, :]
    slot_local = jnp.sum(jnp.where(placed, local_of[:, None] + 1, 0), axis=0) - 1
    place_mat = placed.astype(jnp.bfloat16)
    flat_grad = logit_grad.reshape(-1)
    came_ids = lax.all_to_all(slot_local, "sub", split_axis=0, concat_axis=0, tiled=True)
    select, fetched = node_lookup(came_ids, node_table)
    returned = lax.all_to_all(fetched, "sub", split_axis=0, concat_axis=0, tiled=True)
    pair_nodes = jnp.dot(place_mat, returned, preferred_element_type=jnp.float32).astype(
        jnp.bfloat16
    )
    inputs = jnp.concatenate([jnp.repeat(users, per_row, axis=0), pair_nodes], axis=1)
    pre_grad, in_grad = grad_pass(inputs, flat_grad, w_in, b_in, w_out)
    user_grad = jnp.sum(
        in_grad[:, :user_width].astype(jnp.float32).reshape(row_count, per_row, user_width), axis=1
    )
    slot_back = lead_product(place_mat, in_grad[:, user_width:]).astype(jnp.bfloat16)
    arrived = lax.all_to_all(slot_back, "sub", split_axis=0, concat_axis=0, tiled=True)
    node_part = lead_product(select, arrived)
    weight_part = lax.psum_scatter(
        lead_product(pre_grad, inputs), "sub", scatter_dimension=0, tiled=True
    )
    node_grad, weight_sum = (
        lax.psum(node_part.astype(jnp.bfloat16), "grp").astype(jnp.float32),
        lax.psum(weight_part.astype(jnp.bfloat16), "grp").astype(jnp.float32),
    )
    return (user_grad, node_grad, weight_sum / float(n_sub * n_grp))


def solution(mesh):
    return jax.shard_map(
        local,
        mesh=mesh,
        in_specs=(
            P(("grp", "sub"), None),
            P(("grp", "sub"), None),
            P("sub", None),
            P(),
            P(),
            P(),
            P(("grp", "sub"), None),
        ),
        out_specs=(P(("grp", "sub"), None), P("sub", None), P("sub", None)),
        check_vma=False,
    )
```

profile of v0, /device:TPU:56, one launch (start us, length us, event | category | flops | bytes accessed | tf_op | source)
XLA Modules:
  0.0 298.3 jit_solution(342369465129057940)
XLA Ops:
  8.0 0.9 reshape.117
  9.0 0.6 reduce-window.6
  9.6 0.2 slice_reduce_fusion
  10.3 19.4 %all_to_all.30 = s32[64,7,1]{1,2,0:T(1,128)S(1)} all-to-all(s32[64,7,1]{1,2,0:T(1,128)S(1)} %bitcast.21), channel_id=1, replica_groups=mesh['grp'=12,'sub'=64] {'sub'}, dimensions={0} | all-to-all | bytes 3584 | tf_op jit(solution)/shard_map/all_to_all | solution.py:50
  29.7 0.5 broadcast.150
  30.2 0.7 reduce.5
  31.1 1.4 fusion.3
  32.5 0.7 all_to_all.21
  33.2 7.2 %all-to-all-start.1 = ((bf16[64,7,128]{2,1,0:T(8,128)(2,1)}), bf16[64,7,128]{2,1,0:T(8,128)(2,1)S(1)}, u32[]{:S(2)}, u32[]{:S(2)}) async-start(bf16[64,7,128]{2,1,0:T(8,128)(2,1)} %all_to_all.21), calls=%async_computation.1 | async-start | bytes 262144 | tf_op jit(solution)/shard_map/all_to_all | solution.py:52
  40.5 0.8 reshape.116
  41.4 7.7 %all-to-all-done.1 = bf16[64,7,128]{2,1,0:T(8,128)(2,1)S(1)} async-done(((bf16[64,7,128]{2,1,0:T(8,128)(2,1)}), bf16[64,7,128]{2,1,0:T(8,128)(2,1)S(1)}, u32[]{:S(2)}, u32[]{:S(2)}) %all-to-all-start.1) | async-done | bytes 114720 | tf_op jit(solution)/shard_map/all_to_all | solution.py:52
  49.1 0.3 convolution_convert_fusion.2
  49.4 0.6 copy-done.3
  50.0 2.3 multiply_convert_fusion
  52.3 1.0 convolution_convert_fusion
  53.4 0.7 copy-done.1
  54.1 1.0 convolution_convert_fusion.1
  55.1 1.6 all_to_all.24
  56.7 16.5 %all_to_all.31 = bf16[64,7,128]{2,1,0:T(8,128)(2,1)} all-to-all(bf16[64,7,128]{2,1,0:T(8,128)(2,1)} %all_to_all.24), channel_id=1, replica_groups=mesh['grp'=12,'sub'=64] {'sub'}, dimensions={0} | all-to-all | bytes 229376 | tf_op jit(solution)/shard_map/all_to_all | solution.py:62
  73.2 1.6 all_to_all.26
  74.8 2.4 fusion.2
  77.3 4.3 %fusion.8 = f32[2048,640]{1,0:T(8,128)} fusion(bf16[224,2048]{1,0:T(8,128)(2,1)S(1)} %multiply_convert_fusion, bf16[224,128]{1,0:T(8,128)(2,1)} %copy-done.3, bf16[224,512]{1,0:T(8,128)(2,1)} %reshape.116), kind=kOutput, calls=%fused_computation.18 | convolution fusion | flops 587776000 | bytes 6447104 | tf_op jit(solution)/shard_map/dot_general | solution.py:26
  81.7 0.9 copy-done.2
  82.6 0.8 slice_convert_fusion
  83.4 1.1 reshape.124
  84.5 0.7 reduce_sum.29
  85.2 104.3 %all-reduce.3.cloned.1.call-done = bf16[1024,128]{1,0:T(8,128)(2,1)} async-done(((bf16[1024,128]{1,0:T(8,128)(2,1)}), bf16[1024,128]{1,0:T(8,128)(2,1)}) %all-reduce.3.cloned.1.call-update) | async-done | bytes 262160 | tf_op jit(solution)/shard_map/psum | solution.py:68
  189.5 1.8 convert_element_type.41
  191.3 53.5 %reduce-scatter.2.cloned.1.call-done = f32[32,640]{1,0:T(8,128)} async-done(((f32[2048,640]{1,0:T(8,128)}), f32[32,640]{1,0:T(8,128)}) %reduce-scatter.2.cloned.1.call-update) | async-done | bytes 81936 | tf_op jit(solution)/shard_map/reduce_scatter | solution.py:64
  244.8 0.9 convert_element_type.42
  245.7 44.5 %psum.15 = bf16[32,640]{1,0:T(8,128)(2,1)S(1)} all-reduce(bf16[32,640]{1,0:T(8,128)(2,1)S(1)} %convert_element_type.42), channel_id=1, replica_groups=mesh['grp'=12,'sub'=64] {'grp'}, use_global_device_ids=true, to_apply=%region_7.8 | all-reduce | flops 20480 | bytes 81920 | tf_op jit(solution)/shard_map/psum | solution.py:69
  290.3 0.6 convert_multiply_fusion
  (28 shorter events, 0.9 us)
Async XLA Ops:
  8.0 42.0 %copy-start = (bf16[640,2048]{1,0:T(8,128)(2,1)S(1)}, bf16[640,2048]{1,0:T(8,128)(2,1)}, u32[]{:S(2)}) copy-start(bf16[640,2048]{1,0:T(8,128)(2,1)} %param.10) | copy-start | bytes 7864324
  8.0 32.5 %copy-start.4 = (bf16[16,512]{1,0:T(8,128)(2,1)S(1)}, bf16[16,512]{1,0:T(8,128)(2,1)}, u32[]{:S(2)}) copy-start(bf16[16,512]{1,0:T(8,128)(2,1)} %param.7) | copy-start | bytes 49156
  8.0 33.3 %copy-start.5 = (f32[16,14]{1,0:T(8,128)S(1)}, f32[16,14]{1,0:T(8,128)}, u32[]{:S(2)}) copy-start(f32[16,14]{1,0:T(8,128)} %param.13) | copy-start | bytes 2692
  33.2 15.8 %all-to-all-start.1 = ((bf16[64,7,128]{2,1,0:T(8,128)(2,1)}), bf16[64,7,128]{2,1,0:T(8,128)(2,1)S(1)}, u32[]{:S(2)}, u32[]{:S(2)}) async-start(bf16[64,7,128]{2,1,0:T(8,128)(2,1)} %all_to_all.21), calls=%async_computation.1 | async-start | bytes 262144 | tf_op jit(solution)/shard_map/all_to_all | solution.py:52
  40.4 149.1 %all-reduce.3.cloned.1.call-start = ((), (), s32[]{:S(2)}) async-start(), calls=%async_computation.4 | async-start | bytes 524288 | tf_op jit(solution)/shard_map/psum | solution.py:68
  49.4 0.6 copy-start.3
  53.4 0.7 copy-start.1
  77.3 167.5 %reduce-scatter.2.cloned.1.call-start = ((), (), s32[]{:S(2)}) async-start(), calls=%async_computation.5 | async-start | bytes 5324800 | tf_op jit(solution)/shard_map/reduce_scatter | solution.py:64
  81.6 1.0 copy-start.2
Sparse Core Ops, SparseCore 0:
  77.4 112.1 all-reduce.2
Sparse Core Ops, SparseCore 1:
  83.9 160.9 reduce-scatter.1
where the time goes:
time: 300 us; the launch traced here: 298 us
  waiting for transfers between devices  166 us (55%)
  blocking collectives  80.5 us (27%)
  between operations  15.7 us (5%)
  matrix products  12.8 us (4%)
  local copies, waits for them, and re-layouts  10 us (3%)
  starting transfers between devices  7.26 us (2%)
  other arithmetic  6.53 us (2%)
    psum x1, waiting for transfers between devices, local(): lax.psum(node_part.astype(jnp.bfloat16), 'grp').astype(jnp.float32)  104 us
    reduce_scatter x1, waiting for transfers between devices, local(): lax.psum_scatter(lead_product(pre_grad, inputs), 'sub', scatter_dimension...  53.5 us
    psum x1, blocking collectives, local(): lax.psum(weight_part.astype(jnp.bfloat16), 'grp').astype(jnp.float32)  44.5 us
    all_to_all x1, blocking collectives, local(): lax.all_to_all(slot_local, 'sub', split_axis=0, concat_axis=0, tiled=True)  19.4 us
    all_to_all x1, blocking collectives, local(): lax.all_to_all(slot_back, 'sub', split_axis=0, concat_axis=0, tiled=True)  16.5 us
    dot_general x3, matrix products, lead_product(): lax.dot_general(left, right, (((0,), (0,)), ((), ())), preferred_element_...  7.78 us
    all_to_all x1, waiting for transfers between devices, local(): lax.all_to_all(fetched, 'sub', split_axis=0, concat_axis=0, tiled=True)  7.67 us
    all_to_all x1, starting transfers between devices, local(): lax.all_to_all(fetched, 'sub', split_axis=0, concat_axis=0, tiled=True)  7.18 us
  transfers between devices with their start and end apart: 3, of which 3 were waited for; matrix products, arithmetic and copies ran while one was open for 3% of the time, Pallas kernels for 0%

commit v1 on v0

v1 whole, which is shorter than its diff:
```python
import functools

import jax
import jax.numpy as jnp
from jax import lax
from jax.experimental import pallas as pl
from jax.experimental.pallas import tpu as pltpu
from jax.sharding import PartitionSpec as P

F32 = jnp.float32
BF16 = jnp.bfloat16
SLOTS = 8


def dot(a, b, ca=1, cb=0):
    return lax.dot_general(a, b, (((ca,), (cb,)), ((), ())), preferred_element_type=F32)


def iota(shape, dim):
    return lax.broadcasted_iota(jnp.int32, shape, dim)


def each(n, fn):
    def step(d, carry):
        fn(d)
        return carry

    lax.fori_loop(1, n, step, 0)


def push(src, dst, send_sem, recv_sem, device):
    return pltpu.make_async_remote_copy(
        src_ref=src,
        dst_ref=dst,
        send_sem=send_sem,
        recv_sem=recv_sem,
        device_id=device,
        device_id_type=pl.DeviceIdType.MESH,
    )


def kernel(
    ny, nx, ng,
    ids_ref, users_ref, lg_ref, b_ref, wout_ref, table_hbm, win_hbm,
    ug_ref, ng_ref, w1_ref,
    table, win, place, base, pgs, pn_ref,
    src1, mid1, out1, src2, mid2, out2, src3, mid3, out3,
    urecv, psend, precv, tsend, trecv, qsend, qrecv,
    znode, rnode, anode, bnode, zw, rw, aw, bw,
    load_sem, x_send, x_recv, y_send, y_recv, z_send, z_recv,
):
    rows, per_row = ids_ref.shape
    nodes = table.shape[0]
    width = table.shape[1]
    hid = win.shape[1]
    du = users_ref.shape[1]
    pairs = rows * per_row
    padded = place.shape[0]
    slots = place.shape[1]
    shards = ny * nx
    hb = hid // shards
    band = nx * hb

    g = lax.axis_index("grp")
    me = lax.axis_index("sub")
    y = me // nx
    x = me % nx

    load_table = pltpu.make_async_copy(table_hbm, table, load_sem.at[0])
    load_win = pltpu.make_async_copy(win_hbm, win, load_sem.at[1])
    load_win.start()
    load_table.start()

    def x_peer(d):
        return {"sub": y * nx + (x + d) % nx}

    def y_peer(d):
        return {"sub": ((y + d) % ny) * nx + x}

    def z_peer(d):
        return {"grp": (g + d) % ng}

    barrier = pltpu.get_barrier_semaphore()

    def greet(peer):
        def go(d):
            pl.semaphore_signal(
                barrier, inc=1, device_id=peer(d), device_id_type=pl.DeviceIdType.MESH
            )

        return go

    each(nx, greet(x_peer))
    each(ny, greet(y_peer))
    each(ng, greet(z_peer))

    lanes = 128
    ids = ids_ref[...]
    cols = jnp.concatenate(
        [jnp.broadcast_to(ids[:, k : k + 1], (rows, lanes)) for k in range(per_row)]
        + [jnp.full((padded - pairs, lanes), -1, jnp.int32)],
        axis=0,
    )
    shift = nodes.bit_length() - 1
    owner = lax.shift_right_arithmetic(cols, jnp.int32(shift))
    local = cols & (nodes - 1)
    lane = iota((padded, lanes), 1)
    hit = (owner == lane).astype(F32)
    before = (iota((padded, padded), 0) > iota((padded, padded), 1)).astype(F32).astype(BF16)
    counts = dot(before, hit.astype(BF16))
    rank = jnp.sum(counts * hit, axis=1, keepdims=True)
    code = owner[:, 0:1].astype(F32) * float(SLOTS) + rank
    chosen = (iota((padded, slots), 1).astype(F32) == code).astype(F32).astype(BF16)
    place[...] = chosen
    half = lanes // 2
    asked = jnp.where(
        lane < half, lax.shift_right_arithmetic(local, jnp.int32(5)) + 1, local & 31
    )
    request = dot(chosen, asked.astype(F32).astype(BF16), 0, 0)
    src1[...] = request.reshape(ny, nx, SLOTS, lanes).astype(BF16)

    pl.semaphore_wait(barrier, (nx - 1) + (ny - 1) + (ng - 1))

    def x_stage(num, src, dst):
        return lambda d: push(
            src((x + d) % nx), dst.at[x], x_send.at[num, d], x_recv.at[num, d], x_peer(d)
        )

    def x_arrival(num, src, dst):
        return lambda d: push(
            src(x), dst.at[(x + nx - d) % nx], x_send.at[num, d], x_recv.at[num, d], x_peer(d)
        )

    def y_stage(num, src, dst):
        return lambda d: push(
            src((y + d) % ny), dst.at[y], y_send.at[num, d], y_recv.at[num, d], y_peer(d)
        )

    def y_arrival(num, src, dst):
        return lambda d: push(
            src(y), dst.at[(y + ny - d) % ny], y_send.at[num, d], y_recv.at[num, d], y_peer(d)
        )

    def z_stage(num, src, dst):
        return lambda d: push(
            src((g + d) % ng), dst.at[g], z_send.at[num, d], z_recv.at[num, d], z_peer(d)
        )

    def z_arrival(num, src, dst):
        return lambda d: push(
            src(g), dst.at[(g + ng - d) % ng], z_send.at[num, d], z_recv.at[num, d], z_peer(d)
        )

    def go(n, make):
        each(n, lambda d: make(d).start())

    def come(n, make):
        each(n, lambda d: make(d).wait_recv())

    def gone(n, make):
        each(n, lambda d: make(d).wait_send())

    def by_x(ref):
        return lambda t: ref.at[:, t]

    def by_lead(ref):
        return lambda t: ref.at[t]

    def whole(ref):
        return lambda t: ref

    go(nx, x_stage(0, by_x(src1), mid1))
    mid1[x] = src1[:, x]
    go(nx, x_stage(1, whole(users_ref), urecv))
    urecv[x] = users_ref[...]
    load_win.wait()
    base[...] = dot(users_ref[...], win[0:du, :]) + b_ref[...]
    come(nx, x_arrival(0, by_x(src1), mid1))
    go(ny, y_stage(0, by_x(mid1), out1))
    out1[y] = mid1[:, y]
    load_table.wait()
    come(ny, y_arrival(0, by_x(mid1), out1))

    wanted = out1[...].astype(F32).reshape(slots, lanes)
    place_of = (wanted[:, 0:1] - 1.0) * 32.0 + wanted[:, half : half + 1]
    select = (iota((slots, nodes), 1).astype(F32) == place_of).astype(F32).astype(BF16)
    fetched = dot(select, table[...])
    src2[...] = fetched.reshape(ny, nx, SLOTS, width).astype(BF16)
    go(nx, x_stage(2, by_x(src2), mid2))
    mid2[x] = src2[:, x]
    come(nx, x_arrival(2, by_x(src2), mid2))
    go(ny, y_stage(1, by_x(mid2), out2))
    out2[y] = mid2[:, y]
    come(ny, y_arrival(1, by_x(mid2), out2))

    returned = out2[...].astype(F32).reshape(slots, width).astype(BF16)
    pn = dot(place[0:pairs, :], returned).astype(BF16)
    pn_ref[...] = pn
    grad_col = jnp.concatenate([lg_ref[:, k : k + 1] for k in range(per_row)], axis=0)
    step = min(hid, 512)
    sums = []
    for c in range(0, hid, step):
        cut = slice(c, c + step)
        part = dot(pn, win[du:, cut]).reshape(per_row, rows, step)
        pre = (part + base[:, cut][None]).reshape(pairs, step)
        squash = jax.nn.sigmoid(pre)
        pre_grad = (
            (grad_col * wout_ref[:, cut]) * (squash * (1.0 + pre * (1.0 - squash)))
        ).astype(BF16)
        pgs[:, cut] = pre_grad
        sums.append(jnp.sum(pre_grad.astype(F32).reshape(per_row, rows, step), axis=0))
    in_grad = dot(pgs[...], win[du:, :], 1, 1).astype(BF16)
    back = dot(place[0:pairs, :], in_grad, 0, 0)

    src3[...] = back.reshape(ny, nx, SLOTS, width).astype(BF16)
    go(nx, x_stage(3, by_x(src3), mid3))
    mid3[x] = src3[:, x]

    row_sum = jnp.concatenate(sums, axis=1)
    turned = jnp.concatenate([row_sum[:, j * band : (j + 1) * band] for j in range(ny)], axis=0).T
    for i in range(nx):
        tsend[i] = turned[i * hb : (i + 1) * hb].astype(BF16)
    for j in range(ny):
        prod = dot(pgs[:, j * band : (j + 1) * band], pn_ref[...], 0, 0).astype(BF16)
        for i in range(nx):
            psend[i, j] = prod[i * hb : (i + 1) * hb]

    come(nx, x_arrival(3, by_x(src3), mid3))
    go(ny, y_stage(2, by_x(mid3), out3))
    out3[y] = mid3[:, y]
    go(nx, x_stage(4, by_lead(tsend), trecv))
    go(nx, x_stage(5, by_lead(psend), precv))
    trecv[x] = tsend[x]
    precv[x] = psend[x]
    ug_ref[...] = dot(row_sum.astype(BF16), win[0:du, :], 1, 1)
    come(ny, y_arrival(2, by_x(mid3), out3))

    arrived = out3[...].astype(F32).reshape(slots, width).astype(BF16)
    node_part = dot(select, arrived, 0, 0).astype(BF16)
    zr = znode.shape[1]
    for j in range(ng):
        lo, hi = min(j * zr, nodes), min((j + 1) * zr, nodes)
        if hi > lo:
            znode[j, 0 : hi - lo] = node_part[lo:hi]
        if hi - lo < zr:
            znode[j, hi - lo :] = jnp.zeros((zr - (hi - lo), width), BF16)
    go(ng, z_stage(0, by_lead(znode), rnode))
    rnode[g] = znode[g]

    come(nx, x_arrival(1, whole(users_ref), urecv))
    come(nx, x_arrival(4, by_lead(tsend), trecv))
    come(nx, x_arrival(5, by_lead(psend), precv))
    node_cols = precv[0].astype(F32)
    for i in range(1, nx):
        node_cols += precv[i].astype(F32)
    tl = trecv.shape[2]
    own_row = iota((ny * hb, tl), 0) // hb == iota((ny * hb, tl), 1) // rows
    keep = own_row.astype(F32).astype(BF16)
    left = jnp.concatenate(
        [jnp.concatenate([trecv[i]] * ny, axis=0) * keep for i in range(nx)], axis=1
    )
    right = jnp.concatenate([urecv[i] for i in range(nx) for _ in range(ny)], axis=0)
    user_cols = dot(left, right)
    for j in range(ny):
        qsend[j, :, 0:du] = user_cols[j * hb : (j + 1) * hb].astype(BF16)
        qsend[j, :, du:] = node_cols[j].astype(BF16)
    go(ny, y_stage(3, by_lead(qsend), qrecv))
    qrecv[y] = qsend[y]
    come(ng, z_arrival(0, by_lead(znode), rnode))
    node_sum = rnode[0].astype(F32)
    for j in range(1, ng):
        node_sum += rnode[j].astype(F32)
    bnode[...] = node_sum.astype(BF16)
    go(ng, z_stage(1, whole(bnode), anode))
    anode[g] = bnode[...]

    come(ny, y_arrival(3, by_lead(qsend), qrecv))
    block = qrecv[0].astype(F32)
    for j in range(1, ny):
        block += qrecv[j].astype(F32)
    block = block.astype(BF16)
    across = (du + width) // lanes
    tiles = [(a, c) for a in range(hb // 16) for c in range(across)]
    per = zw.shape[1] // 16
    for n in range(ng * per):
        at = (n // per, slice((n % per) * 16, (n % per) * 16 + 16))
        if n < len(tiles):
            a, c = tiles[n]
            zw[at] = block[a * 16 : a * 16 + 16, c * lanes : (c + 1) * lanes]
        else:
            zw[at] = jnp.zeros((16, lanes), BF16)
    go(ng, z_stage(2, by_lead(zw), rw))
    rw[g] = zw[g]
    come(ng, z_arrival(2, by_lead(zw), rw))
    tile_sum = rw[0].astype(F32)
    for j in range(1, ng):
        tile_sum += rw[j].astype(F32)
    bw[...] = tile_sum.astype(BF16)
    go(ng, z_stage(3, whole(bw), aw))
    aw[g] = bw[...]

    come(ng, z_arrival(1, whole(bnode), anode))
    for j in range(ng):
        lo, hi = min(j * zr, nodes), min((j + 1) * zr, nodes)
        if hi > lo:
            ng_ref[lo:hi] = anode[j, 0 : hi - lo].astype(F32)
    come(ng, z_arrival(3, whole(bw), aw))
    devices = float(shards * ng)
    for n, (a, c) in enumerate(tiles):
        at = (n // per, slice((n % per) * 16, (n % per) * 16 + 16))
        w1_ref[a * 16 : a * 16 + 16, c * lanes : (c + 1) * lanes] = aw[at].astype(F32) / devices

    gone(nx, x_stage(0, by_x(src1), mid1))
    gone(nx, x_stage(1, whole(users_ref), urecv))
    gone(nx, x_stage(2, by_x(src2), mid2))
    gone(nx, x_stage(3, by_x(src3), mid3))
    gone(nx, x_stage(4, by_lead(tsend), trecv))
    gone(nx, x_stage(5, by_lead(psend), precv))
    gone(ny, y_stage(0, by_x(mid1), out1))
    gone(ny, y_stage(1, by_x(mid2), out2))
    gone(ny, y_stage(2, by_x(mid3), out3))
    gone(ny, y_stage(3, by_lead(qsend), qrecv))
    gone(ng, z_stage(0, by_lead(znode), rnode))
    gone(ng, z_stage(1, whole(bnode), anode))
    gone(ng, z_stage(2, by_lead(zw), rw))
    gone(ng, z_stage(3, whole(bw), aw))


def local(ng, shards, users, node_ids, node_table, w_in, b_in, w_out, logit_grad):
    nx = 8 if shards > 8 and shards % 8 == 0 else 2
    ny = shards // nx
    rows, per_row = node_ids.shape
    du = users.shape[1]
    nodes, width = node_table.shape
    din, hid = w_in.shape
    pairs = rows * per_row
    padded = -(-pairs // 128) * 128
    slots = shards * SLOTS
    hb = hid // shards
    zr = -(-nodes // (ng * 16)) * 16
    tiles = (hb // 16) * (din // 128)
    zt = -(-tiles // ng) * 16
    vmem, hbm = pl.BlockSpec(memory_space=pltpu.VMEM), pl.BlockSpec(memory_space=pl.ANY)

    def ex():
        return [
            pltpu.VMEM((ny, nx, SLOTS, width), BF16),
            pltpu.VMEM((nx, ny, SLOTS, width), BF16),
            pltpu.VMEM((ny, nx, SLOTS, width), BF16),
        ]

    return pl.pallas_call(
        functools.partial(kernel, ny, nx, ng),
        out_shape=(
            jax.ShapeDtypeStruct((rows, du), F32),
            jax.ShapeDtypeStruct((nodes, width), F32),
            jax.ShapeDtypeStruct((hb, din), F32),
        ),
        in_specs=[vmem] * 5 + [hbm] * 2,
        out_specs=(vmem, vmem, vmem),
        scratch_shapes=[
            pltpu.VMEM((nodes, width), BF16),
            pltpu.VMEM((din, hid), BF16),
            pltpu.VMEM((padded, slots), BF16),
            pltpu.VMEM((rows, hid), F32),
            pltpu.VMEM((pairs, hid), BF16),
            pltpu.VMEM((pairs, width), BF16),
            *ex(), *ex(), *ex(),
            pltpu.VMEM((nx, rows, du), BF16),
            pltpu.VMEM((nx, ny, hb, width), BF16),
            pltpu.VMEM((nx, ny, hb, width), BF16),
            pltpu.VMEM((nx, hb, ny * rows), BF16),
            pltpu.VMEM((nx, hb, ny * rows), BF16),
            pltpu.VMEM((ny, hb, din), BF16),
            pltpu.VMEM((ny, hb, din), BF16),
            pltpu.VMEM((ng, zr, width), BF16),
            pltpu.VMEM((ng, zr, width), BF16),
            pltpu.VMEM((ng, zr, width), BF16),
            pltpu.VMEM((zr, width), BF16),
            pltpu.VMEM((ng, zt, 128), BF16),
            pltpu.VMEM((ng, zt, 128), BF16),
            pltpu.VMEM((ng, zt, 128), BF16),
            pltpu.VMEM((zt, 128), BF16),
            pltpu.SemaphoreType.DMA((2,)),
            pltpu.SemaphoreType.DMA((6, nx)),
            pltpu.SemaphoreType.DMA((6, nx)),
            pltpu.SemaphoreType.DMA((4, ny)),
            pltpu.SemaphoreType.DMA((4, ny)),
            pltpu.SemaphoreType.DMA((4, ng)),
            pltpu.SemaphoreType.DMA((4, ng)),
        ],
        compiler_params=pltpu.CompilerParams(
            collective_id=0, has_side_effects=True, vmem_limit_bytes=40 * 2**20
        ),
    )(
        node_ids, users, logit_grad, b_in.reshape(1, hid), w_out.reshape(1, hid),
        node_table, w_in,
    )


def solution(mesh):
    ng, shards = mesh.shape["grp"], mesh.shape["sub"]
    return jax.shard_map(
        functools.partial(local, ng, shards),
        mesh=mesh,
        in_specs=(
            P(("grp", "sub"), None),
            P(("grp", "sub"), None),
            P("sub", None),
            P(),
            P(),
            P(),
            P(("grp", "sub"), None),
        ),
        out_specs=(P(("grp", "sub"), None), P("sub", None), P("sub", None)),
        check_vma=False,
    )
```

time: 300 us -> 97.5 us (0.33)
  the two profiles are of different devices: /device:TPU:56 before, /device:TPU:64 now
where the time goes in v1:
time: 97.5 us; the launch traced here: 97 us
  Pallas kernels  88.1 us (90%)
  local copies, waits for them, and re-layouts  8.23 us (8%)
    pallas_call x1, Pallas kernels, local(): pl.pallas_call(functools.partial(kernel, ny, nx, ng), out_shape=(jax.Shap...  88.1 us
    unnamed x17, local copies, waits for them, and re-layouts  8.23 us

profile of v1, /device:TPU:64, one launch (start us, length us, event | category | flops | bytes accessed | tf_op | source)
XLA Modules:
  0.0 97.0 jit_solution(199171345060809259)
XLA Ops:
  0.6 0.0 copy-start
  0.6 1.7 %copy-done = bf16[640,2048]{1,0:T(8,128)(2,1)S(1)} copy-done((bf16[640,2048]{1,0:T(8,128)(2,1)S(1)}, bf16[640,2048]{1,0:T(8,128)(2,1)}, u32[]{:S(2)}) %copy-start) | copy-done | bytes 2621464
  2.4 0.0 copy-start.1
  2.4 0.9 copy-done.1
  3.3 0.0 copy-start.2
  3.3 0.7 copy-done.2
  4.0 0.0 copy-start.3
  4.0 0.7 copy-done.3
  4.7 0.0 copy-start.4
  4.7 0.7 copy-done.4
  5.4 0.0 copy-start.5
  5.4 0.7 copy-done.5
  6.1 0.0 copy-start.6
  6.1 0.7 copy-done.6
  6.8 88.1 %shard_map.94 = (f32[16,512]{1,0:T(8,128)S(1)}, f32[1024,128]{1,0:T(8,128)S(1)}, f32[32,640]{1,0:T(8,128)S(1)}) custom-call(s32[16,14]{1,0:T(8,128)S(1)} %copy-done.3, bf16[16,512]{1,0:T(8,128)(2,1)S(1)} %copy-done.2, f32[16,14]{1,0:T(8,128)S(1)} %copy-done.4, f32[1,2048]{1,0:T(1,128)S(1)} %bitcast.2, f32[1,2048]{1,0:T(1,128)S(1)} %bitcast.3, ...), custom_call_target="tpu_custom_call" | custom-call | tf_op jit(solution)/shard_map/pallas_call | solution.py:352
  95.0 0.6 copy.13
  95.6 0.8 copy.14
  96.4 0.6 copy.15
Async XLA Ops:
  0.6 1.7 %copy-start = (bf16[640,2048]{1,0:T(8,128)(2,1)S(1)}, bf16[640,2048]{1,0:T(8,128)(2,1)}, u32[]{:S(2)}) copy-start(bf16[640,2048]{1,0:T(8,128)(2,1)} %win_hbm.1) | copy-start | bytes 7864324
  2.4 0.9 copy-start.1
  3.3 0.7 copy-start.2
  4.0 0.7 copy-start.3
  4.7 0.7 copy-start.4
  5.4 0.7 copy-start.5
  6.1 0.7 copy-start.6

commit v2 on v1

v2 whole, which is shorter than its diff:
```python
import functools

import jax
import jax.numpy as jnp
from jax import lax
from jax.experimental import pallas as pl
from jax.experimental.pallas import tpu as pltpu
from jax.sharding import PartitionSpec as P

F32 = jnp.float32
BF16 = jnp.bfloat16
SLOTS = 8


def dot(a, b, ca=1, cb=0):
    return lax.dot_general(a, b, (((ca,), (cb,)), ((), ())), preferred_element_type=F32)


def iota(shape, dim):
    return lax.broadcasted_iota(jnp.int32, shape, dim)


def each(n, fn):
    def step(d, carry):
        fn(d)
        return carry

    lax.fori_loop(1, n, step, 0)


def push(src, dst, send_sem, recv_sem, device):
    return pltpu.make_async_remote_copy(
        src_ref=src,
        dst_ref=dst,
        send_sem=send_sem,
        recv_sem=recv_sem,
        device_id=device,
        device_id_type=pl.DeviceIdType.MESH,
    )


def kernel(
    ny, nx, ng,
    ids_hbm, users_hbm, lg_hbm, b_hbm, wout_hbm, table_hbm, win_hbm,
    ug_ref, anode, aw,
    ids_ref, users_ref, lg_ref, b_ref, wout_ref, table, win,
    place, place_t, select_t, right, base, pgs,
    src1, out1, src2, out2, src3, out3,
    urecv, psend, precv, tsend, trecv, qusend, qurecv, qnsend, qnrecv,
    znode, nrecv, hsum, frecv, bnode, afar, zw, rw, bw,
    load_sem, own_sem, d_send, d_recv, x_send, x_recv, y_send, y_recv, z_send, z_recv,
    zn_send, zn_recv, zf_send, zf_recv,
):
    rows, per_row = ids_ref.shape
    nodes = table.shape[0]
    width = table.shape[1]
    hid = win.shape[1]
    du = users_ref.shape[1]
    pairs = rows * per_row
    padded = place.shape[0]
    slots = place.shape[1]
    shards = ny * nx
    hb = hid // shards
    band = nx * hb

    g = lax.axis_index("grp")
    me = lax.axis_index("sub")
    y = me // nx
    x = me % nx

    loads = [
        pltpu.make_async_copy(src, dst, load_sem.at[n])
        for n, (src, dst) in enumerate(
            [
                (ids_hbm, ids_ref),
                (users_hbm, users_ref),
                (win_hbm, win),
                (table_hbm, table),
                (b_hbm, b_ref),
                (wout_hbm, wout_ref),
                (lg_hbm, lg_ref),
            ]
        )
    ]
    for load in loads:
        load.start()
    load_ids, load_users, load_win, load_table, *load_small = loads

    def x_peer(d):
        return {"sub": y * nx + (x + d) % nx}

    def y_peer(d):
        return {"sub": ((y + d) % ny) * nx + x}

    def sub_peer(d):
        return {"sub": (me + d) % shards}

    def z_peer(d):
        return {"grp": (g + d) % ng}

    barrier = pltpu.get_barrier_semaphore()

    def greet(peer):
        def go(d):
            pl.semaphore_signal(
                barrier, inc=1, device_id=peer(d), device_id_type=pl.DeviceIdType.MESH
            )

        return go

    each(shards, greet(sub_peer))
    each(ng, greet(z_peer))

    lanes = 128
    half = lanes // 2
    load_ids.wait()
    ids = ids_ref[...]
    cols = jnp.concatenate(
        [jnp.broadcast_to(ids[:, k : k + 1], (rows, lanes)) for k in range(per_row)]
        + [jnp.full((padded - pairs, lanes), -1, jnp.int32)],
        axis=0,
    )
    shift = nodes.bit_length() - 1
    owner = lax.shift_right_arithmetic(cols, jnp.int32(shift))
    local = cols & (nodes - 1)
    lane = iota((padded, lanes), 1)
    hit = (owner == lane).astype(F32)
    hit_low = hit.astype(BF16)
    before = (iota((padded, padded), 0) > iota((padded, padded), 1)).astype(F32).astype(BF16)
    rank = jnp.sum(dot(before, hit_low) * hit, axis=1, keepdims=True)
    slot_lane = rank.astype(jnp.int32)
    high, low = lax.shift_right_arithmetic(local, jnp.int32(5)) + 1, local & 31
    asked = jnp.where(lane == slot_lane, high, jnp.where(lane == slot_lane + half, low, 0))
    request = dot(hit_low, asked.astype(F32).astype(BF16), 0, 0)
    src1[...] = request[0:shards].reshape(shards, 1, lanes)

    pl.semaphore_wait(barrier, (shards - 1) + (ng - 1))

    def x_stage(num, src, dst):
        return lambda d: push(
            src((x + d) % nx), dst.at[x], x_send.at[num, d], x_recv.at[num, d], x_peer(d)
        )

    def x_arrival(num, src, dst):
        return lambda d: push(
            src(x), dst.at[(x + nx - d) % nx], x_send.at[num, d], x_recv.at[num, d], x_peer(d)
        )

    def y_stage(num, src, dst):
        return lambda d: push(
            src((y + d) % ny), dst.at[y], y_send.at[num, d], y_recv.at[num, d], y_peer(d)
        )

    def y_arrival(num, src, dst):
        return lambda d: push(
            src(y), dst.at[(y + ny - d) % ny], y_send.at[num, d], y_recv.at[num, d], y_peer(d)
        )

    def z_stage(num, src, dst):
        return lambda d: push(
            src((g + d) % ng), dst.at[g], z_send.at[num, d], z_recv.at[num, d], z_peer(d)
        )

    def z_arrival(num, src, dst):
        return lambda d: push(
            src(g), dst.at[(g + ng - d) % ng], z_send.at[num, d], z_recv.at[num, d], z_peer(d)
        )

    def d_stage(num, src, dst):
        return lambda d: push(
            src.at[(me + d) % shards], dst.at[me], d_send.at[num], d_recv.at[num], sub_peer(d)
        )

    def d_all(num, src, dst):
        rest = pl.ds(0, shards - 1)
        return push(src.at[rest], dst.at[rest], d_send.at[num], d_recv.at[num], sub_peer(1))

    def go(n, make):
        each(n, lambda d: make(d).start())

    def come(n, make):
        each(n, lambda d: make(d).wait_recv())

    def gone(n, make):
        each(n, lambda d: make(d).wait_send())

    def by_lead(ref):
        return lambda t: ref.at[t]

    def by_part(ref, h, size):
        return lambda t: ref.at[t, h * size : (h + 1) * size]

    def whole(ref):
        return lambda t: ref

    go(shards, d_stage(0, src1, out1))
    out1[me] = src1[me]
    code = owner[:, 0:1].astype(F32) * float(SLOTS) + rank
    chosen = (iota((padded, slots), 1).astype(F32) == code).astype(F32)
    place[...] = chosen.astype(BF16)
    place_t[...] = chosen.T.astype(BF16)
    slot_row = iota((slots, lanes), 0) % SLOTS
    slot_col = iota((slots, lanes), 1)
    weight = jnp.where(slot_col == slot_row, 32.0, 0.0)
    weight = weight + jnp.where(slot_col == slot_row + half, 1.0, 0.0)
    spread = (iota((slots, shards), 0) // SLOTS == iota((slots, shards), 1)).astype(F32)
    load_users.wait()
    go(nx, x_stage(0, whole(users_ref), urecv))
    urecv[x] = users_ref[...]
    load_win.wait()
    for load in load_small:
        load.wait()
    base[...] = dot(users_ref[...], win[0:du, :]) + b_ref[...]
    load_table.wait()
    d_all(0, src1, out1).wait_recv()

    wanted = dot(spread.astype(BF16), out1[...].reshape(shards, lanes).astype(BF16))
    place_of = jnp.sum(wanted * weight, axis=1, keepdims=True) - 32.0
    select = (iota((slots, nodes), 1).astype(F32) == place_of).astype(F32)
    fetched = dot(select.astype(BF16), table[...])
    src2[...] = fetched.reshape(shards, SLOTS, width).astype(BF16)
    go(shards, d_stage(1, src2, out2))
    out2[me] = src2[me]
    select_t[...] = select.T.astype(BF16)
    come(nx, x_arrival(0, whole(users_ref), urecv))
    for i in range(nx):
        for j in range(ny):
            at = (i * ny + j) * rows
            right[at : at + rows] = urecv[i]
    d_all(1, src2, out2).wait_recv()

    returned = out2[...].astype(F32).reshape(slots, width).astype(BF16)
    pn = dot(place[0:pairs, :], returned).astype(BF16)
    grad_col = jnp.concatenate([lg_ref[:, k : k + 1] for k in range(per_row)], axis=0)
    step = min(hid, 512)
    sums = []
    for c in range(0, hid, step):
        cut = slice(c, c + step)
        part = dot(pn, win[du:, cut]).reshape(per_row, rows, step)
        pre = (part + base[:, cut][None]).reshape(pairs, step)
        squash = jax.nn.sigmoid(pre)
        pre_grad = (
            (grad_col * wout_ref[:, cut]) * (squash * (1.0 + pre * (1.0 - squash)))
        ).astype(BF16)
        pgs[:, cut] = pre_grad
        sums.append(jnp.sum(pre_grad.astype(F32).reshape(per_row, rows, step), axis=0))
    in_grad = dot(pgs[...], win[du:, :], 1, 1).astype(BF16)
    back = dot(place_t[:, 0:pairs], in_grad)

    src3[...] = back.reshape(shards, SLOTS, width).astype(BF16)
    go(shards, d_stage(2, src3, out3))
    out3[me] = src3[me]

    row_sum = jnp.concatenate(sums, axis=1)
    turned = jnp.concatenate([row_sum[:, j * band : (j + 1) * band] for j in range(ny)], axis=0).T
    for i in range(nx):
        tsend[i] = turned[i * hb : (i + 1) * hb].astype(BF16)
    go(nx, x_stage(1, by_lead(tsend), trecv))
    trecv[x] = tsend[x]

    pn_t = pn.astype(F32).T.astype(BF16)
    parts = 2 if ny % 2 == 0 else 1
    bands = ny // parts
    for h in range(parts):
        for j in range(h * bands, (h + 1) * bands):
            prod = dot(pn_t, pgs[:, j * band : (j + 1) * band]).T
            for i in range(nx):
                psend[i, j] = prod[i * hb : (i + 1) * hb].astype(BF16)
        go(nx, x_stage(2 + h, by_part(psend, h, bands), precv.at[:, h * bands : (h + 1) * bands]))
    precv[x] = psend[x]

    d_all(2, src3, out3).wait_recv()
    arrived = out3[...].astype(F32).reshape(slots, width).astype(BF16)
    node_part = dot(select_t[...], arrived).reshape(nodes // 8, 8, width).astype(BF16)
    cls, nf, zu = znode.shape[0:3]
    units = nodes // 8
    for o in range(ng):
        lo, hi = min(o * zu, units), min((o + 1) * zu, units)
        if hi > lo:
            znode[o % cls, o // cls, 0 : hi - lo] = node_part[lo:hi]
        if hi - lo < zu:
            znode[o % cls, o // cls, hi - lo :] = jnp.zeros((zu - (hi - lo), 8, width), BF16)
    near = (1, ng - 1) if cls > 1 else ()
    gc, gi = g % cls, g // cls
    order = [f for f in (2, 1, 3) if f < nf] + [f for f in range(4, nf)] + [0]

    def near_to(k):
        return (g + near[k]) % ng

    def near_from(k):
        return (g + ng - near[k]) % ng

    def rs_near(k, f, to):
        there = near_to(k) if to else g
        at = (there // cls + f) % nf
        return push(
            znode.at[there % cls, at], nrecv.at[k, at],
            zn_send.at[0, k, f], zn_recv.at[0, k, f], {"grp": near_to(k)},
        )

    def rs_far(f):
        return push(
            hsum.at[(gi + f) % nf], frecv.at[f],
            zf_send.at[0, f], zf_recv.at[0, f], {"grp": (g + cls * f) % ng},
        )

    def ag_far(f):
        return push(
            bnode, afar.at[f], zf_send.at[1, f], zf_recv.at[1, f], {"grp": (g + cls * f) % ng}
        )

    def ag_near(k, f, to):
        origin = g if to else near_from(k)
        at = (origin // cls + nf - f) % nf
        return push(
            bnode if f == 0 else afar.at[f], anode.at[origin % cls, at],
            zn_send.at[1, k, f], zn_recv.at[1, k, f], {"grp": near_to(k)},
        )

    for f in order:
        for k in range(len(near)):
            rs_near(k, f, True).start()

    come(nx, x_arrival(1, by_lead(tsend), trecv))
    tl = trecv.shape[2]
    own_row = iota((ny * hb, tl), 0) // hb == iota((ny * hb, tl), 1) // rows
    keep = own_row.astype(F32).astype(BF16)
    left = jnp.concatenate(
        [jnp.concatenate([trecv[i]] * ny, axis=0) * keep for i in range(nx)], axis=1
    )
    user_cols = dot(left, right[...]).astype(BF16)
    for j in range(ny):
        qusend[j] = user_cols[j * hb : (j + 1) * hb]
    go(ny, y_stage(0, by_lead(qusend), qurecv))
    qurecv[y] = qusend[y]

    for f in order:
        at = (gi + f) % nf
        mine = znode[gc, at].astype(F32)
        for k in range(len(near)):
            rs_near(k, f, False).wait_recv()
            mine = mine + nrecv[k, at].astype(F32)
        if f > 0:
            hsum[at] = mine.astype(BF16)
            rs_far(f).start()

    for h in range(parts):
        come(nx, x_arrival(2 + h, by_part(psend, h, bands), precv.at[:, h * bands : (h + 1) * bands]))
    for j in range(ny):
        node_cols = precv[0, j].astype(F32)
        for i in range(1, nx):
            node_cols = node_cols + precv[i, j].astype(F32)
        qnsend[j] = node_cols.astype(BF16)
    go(ny, y_stage(1, by_lead(qnsend), qnrecv))
    qnrecv[y] = qnsend[y]

    for f in range(1, nf):
        rs_far(f).wait_recv()
        mine = mine + frecv[f].astype(F32)
    bnode[...] = mine.astype(BF16)
    for f in order[:-1]:
        ag_far(f).start()
    for k in range(len(near)):
        ag_near(k, 0, True).start()
    keep_own = pltpu.make_async_copy(bnode, anode.at[gc, gi], own_sem.at[0])
    keep_own.start()

    ug_ref[...] = dot(row_sum.astype(BF16), win[0:du, :], 1, 1)
    come(ny, y_arrival(0, by_lead(qusend), qurecv))
    come(ny, y_arrival(1, by_lead(qnsend), qnrecv))
    user_block = qurecv[0].astype(F32)
    node_block = qnrecv[0].astype(F32)
    for j in range(1, ny):
        user_block = user_block + qurecv[j].astype(F32)
        node_block = node_block + qnrecv[j].astype(F32)
    block = jnp.concatenate([user_block, node_block], axis=1).astype(BF16)
    tiles = w1_tiles(hb, du + width)
    per = zw.shape[1] // 16
    for n in range(ng * per):
        at = (n // per, slice((n % per) * 16, (n % per) * 16 + 16))
        if n < len(tiles):
            a, c = tiles[n]
            zw[at] = block[a * 16 : a * 16 + 16, c * lanes : (c + 1) * lanes]
        else:
            zw[at] = jnp.zeros((16, lanes), BF16)
    go(ng, z_stage(0, by_lead(zw), rw))
    rw[g] = zw[g]

    keep_far = []
    for f in order[:-1]:
        ag_far(f).wait_recv()
        for k in range(len(near)):
            ag_near(k, f, True).start()
        copy = pltpu.make_async_copy(
            afar.at[f], anode.at[gc, (gi + nf - f) % nf], own_sem.at[1 + f]
        )
        copy.start()
        keep_far.append(copy)

    come(ng, z_arrival(0, by_lead(zw), rw))
    tile_sum = rw[0].astype(F32)
    for j in range(1, ng):
        tile_sum = tile_sum + rw[j].astype(F32)
    bw[...] = tile_sum.astype(BF16)
    go(ng, z_stage(1, whole(bw), aw))
    keep_w = pltpu.make_async_copy(bw, aw.at[g], own_sem.at[1])
    keep_w.start()

    for f in order:
        for k in range(len(near)):
            ag_near(k, f, False).wait_recv()
    come(ng, z_arrival(1, whole(bw), aw))
    keep_own.wait()
    keep_w.wait()
    for copy in keep_far:
        copy.wait()

    for f in order:
        for k in range(len(near)):
            rs_near(k, f, True).wait_send()
            ag_near(k, f, True).wait_send()
    for f in range(1, nf):
        rs_far(f).wait_send()
        ag_far(f).wait_send()
    d_all(0, src1, out1).wait_send()
    d_all(1, src2, out2).wait_send()
    d_all(2, src3, out3).wait_send()
    gone(nx, x_stage(0, whole(users_ref), urecv))
    gone(nx, x_stage(1, by_lead(tsend), trecv))
    for h in range(parts):
        gone(nx, x_stage(2 + h, by_part(psend, h, bands), precv.at[:, h * bands : (h + 1) * bands]))
    gone(ny, y_stage(0, by_lead(qusend), qurecv))
    gone(ny, y_stage(1, by_lead(qnsend), qnrecv))
    gone(ng, z_stage(0, by_lead(zw), rw))
    gone(ng, z_stage(1, whole(bw), aw))


def finish(
    devices, ug_hbm, node_hbm, w1_hbm, ug_out, node_out, w1_out,
    ug, node_in, w1_in, node, w1, in_sem, out_sem,
):
    cls, nf, zu, _, width = node_in.shape
    units, (hb, din) = node.shape[0] // 8, w1.shape
    loads = [
        pltpu.make_async_copy(src, dst, in_sem.at[n])
        for n, (src, dst) in enumerate([(node_hbm, node_in), (w1_hbm, w1_in), (ug_hbm, ug)])
    ]
    stores = [
        pltpu.make_async_copy(src, dst, out_sem.at[n])
        for n, (src, dst) in enumerate([(node, node_out), (w1, w1_out), (ug, ug_out)])
    ]
    for load in loads:
        load.start()
    loads[0].wait()
    for o in range(cls * nf):
        lo, hi = min(o * zu, units), min((o + 1) * zu, units)
        if hi > lo:
            part = node_in[o % cls, o // cls, 0 : hi - lo].astype(F32)
            node[lo * 8 : hi * 8] = part.reshape((hi - lo) * 8, width)
    stores[0].start()
    loads[2].wait()
    stores[2].start()
    loads[1].wait()
    per = w1_in.shape[1] // 16
    for n, (a, c) in enumerate(w1_tiles(hb, din)):
        part = w1_in[n // per, (n % per) * 16 : (n % per) * 16 + 16].astype(F32)
        w1[a * 16 : a * 16 + 16, c * 128 : (c + 1) * 128] = part / devices
    stores[1].start()
    for store in stores:
        store.wait()


def w1_tiles(hb, din):
    return [(a, c) for a in range(hb // 16) for c in range(din // 128)]


def local(ng, shards, users, node_ids, node_table, w_in, b_in, w_out, logit_grad):
    nx = 8 if shards > 8 and shards % 8 == 0 else 2
    ny = shards // nx
    rows, per_row = node_ids.shape
    du = users.shape[1]
    nodes, width = node_table.shape
    din, hid = w_in.shape
    pairs = rows * per_row
    padded = -(-pairs // 128) * 128
    slots = shards * SLOTS
    hb = hid // shards
    cls = 3 if ng % 3 == 0 and ng > 3 else 1
    nf = ng // cls
    zu = -(-nodes // (ng * 8))
    kn = 2 if cls > 1 else 1
    zt = -(-len(w1_tiles(hb, din)) // ng) * 16
    vmem, hbm = pl.BlockSpec(memory_space=pltpu.VMEM), pl.BlockSpec(memory_space=pltpu.HBM)

    parts = pl.pallas_call(
        functools.partial(kernel, ny, nx, ng),
        out_shape=(
            jax.ShapeDtypeStruct((rows, du), F32),
            jax.ShapeDtypeStruct((cls, nf, zu, 8, width), BF16),
            jax.ShapeDtypeStruct((ng, zt, 128), BF16),
        ),
        in_specs=[hbm] * 7,
        out_specs=(vmem, hbm, hbm),
        scratch_shapes=[
            pltpu.VMEM((rows, per_row), jnp.int32),
            pltpu.VMEM((rows, du), BF16),
            pltpu.VMEM((rows, per_row), F32),
            pltpu.VMEM((1, hid), F32),
            pltpu.VMEM((1, hid), F32),
            pltpu.VMEM((nodes, width), BF16),
            pltpu.VMEM((din, hid), BF16),
            pltpu.VMEM((padded, slots), BF16),
            pltpu.VMEM((slots, padded), BF16),
            pltpu.VMEM((nodes, slots), BF16),
            pltpu.VMEM((shards * rows, du), BF16),
            pltpu.VMEM((rows, hid), F32),
            pltpu.VMEM((pairs, hid), BF16),
            *[pltpu.VMEM((shards, 1, 128), F32)] * 2,
            *[pltpu.VMEM((shards, SLOTS, width), BF16)] * 4,
            pltpu.VMEM((nx, rows, du), BF16),
            *[pltpu.VMEM((nx, ny, hb, width), BF16)] * 2,
            *[pltpu.VMEM((nx, hb, ny * rows), BF16)] * 2,
            *[pltpu.VMEM((ny, hb, du), BF16)] * 2,
            *[pltpu.VMEM((ny, hb, width), BF16)] * 2,
            pltpu.VMEM((cls, nf, zu, 8, width), BF16),
            pltpu.VMEM((kn, nf, zu, 8, width), BF16),
            pltpu.VMEM((nf, zu, 8, width), BF16),
            pltpu.VMEM((nf, zu, 8, width), BF16),
            pltpu.VMEM((zu, 8, width), BF16),
            pltpu.VMEM((nf, zu, 8, width), BF16),
            pltpu.VMEM((ng, zt, 128), BF16),
            pltpu.VMEM((ng, zt, 128), BF16),
            pltpu.VMEM((zt, 128), BF16),
            pltpu.SemaphoreType.DMA((7,)),
            pltpu.SemaphoreType.DMA((1 + nf,)),
            pltpu.SemaphoreType.DMA((3,)),
            pltpu.SemaphoreType.DMA((3,)),
            pltpu.SemaphoreType.DMA((4, nx)),
            pltpu.SemaphoreType.DMA((4, nx)),
            pltpu.SemaphoreType.DMA((2, ny)),
            pltpu.SemaphoreType.DMA((2, ny)),
            pltpu.SemaphoreType.DMA((2, ng)),
            pltpu.SemaphoreType.DMA((2, ng)),
            pltpu.SemaphoreType.DMA((2, kn, nf)),
            pltpu.SemaphoreType.DMA((2, kn, nf)),
            pltpu.SemaphoreType.DMA((2, nf)),
            pltpu.SemaphoreType.DMA((2, nf)),
        ],
        compiler_params=pltpu.CompilerParams(
            collective_id=0, has_side_effects=True, vmem_limit_bytes=60 * 2**20
        ),
    )(
        node_ids, users, logit_grad, b_in.reshape(1, hid), w_out.reshape(1, hid),
        node_table, w_in,
    )
    return pl.pallas_call(
        functools.partial(finish, float(shards * ng)),
        out_shape=(
            jax.ShapeDtypeStruct((rows, du), F32),
            jax.ShapeDtypeStruct((nodes, width), F32),
            jax.ShapeDtypeStruct((hb, din), F32),
        ),
        in_specs=[hbm] * 3,
        out_specs=(hbm, hbm, hbm),
        scratch_shapes=[
            pltpu.VMEM((rows, du), F32),
            pltpu.VMEM((cls, nf, zu, 8, width), BF16),
            pltpu.VMEM((ng, zt, 128), BF16),
            pltpu.VMEM((nodes, width), F32),
            pltpu.VMEM((hb, din), F32),
            pltpu.SemaphoreType.DMA((3,)),
            pltpu.SemaphoreType.DMA((3,)),
        ],
        compiler_params=pltpu.CompilerParams(vmem_limit_bytes=60 * 2**20),
    )(*parts)


def solution(mesh):
    ng, shards = mesh.shape["grp"], mesh.shape["sub"]
    return jax.shard_map(
        functools.partial(local, ng, shards),
        mesh=mesh,
        in_specs=(
            P(("grp", "sub"), None),
            P(("grp", "sub"), None),
            P("sub", None),
            P(),
            P(),
            P(),
            P(("grp", "sub"), None),
        ),
        out_specs=(P(("grp", "sub"), None), P("sub", None), P("sub", None)),
        check_vma=False,
    )
```

time: 97.5 us -> 72.9 us (0.75)
  the two profiles are of different devices: /device:TPU:64 before, /device:TPU:2 now
where the time goes in v2:
time: 72.9 us; the launch traced here: 72.8 us
  Pallas kernels  72.1 us (99%)
    pallas_call x1, Pallas kernels, local(): pl.pallas_call(functools.partial(kernel, ny, nx, ng), out_shape=(jax.Shap...  70.3 us
    pallas_call x1, Pallas kernels, local(): pl.pallas_call(functools.partial(finish, float(shards * ng)), out_shape=(...  1.86 us

profile of v2, /device:TPU:2, one launch (start us, length us, event | category | flops | bytes accessed | tf_op | source)
XLA Modules:
  0.0 72.8 jit_solution(2645459026726763992)
XLA Ops:
  0.6 70.3 %shard_map.94 = (f32[16,512]{1,0:T(8,128)}, bf16[3,4,11,8,128]{4,3,2,1,0:T(8,128)(2,1)}, bf16[12,16,128]{2,1,0:T(8,128)(2,1)}) custom-call(s32[16,14]{1,0:T(8,128)} %ids_hbm.1, bf16[16,512]{1,0:T(8,128)(2,1)} %users_hbm.1, f32[16,14]{1,0:T(8,128)} %lg_hbm.1, f32[1,2048]{1,0:T(1,128)} %bitcast.2, f32[1,2048]{1,0:T(1,128)} %bitcast.3, ...), custom_call_target="tpu_custom_call" | custom-call | tf_op jit(solution)/shard_map/pallas_call | solution.py:495
  70.9 1.9 %shard_map.95 = (f32[16,512]{1,0:T(8,128)}, f32[1024,128]{1,0:T(8,128)}, f32[32,640]{1,0:T(8,128)}) custom-call(f32[16,512]{1,0:T(8,128)} %get-tuple-element.6.ug_hbm, bf16[3,4,11,8,128]{4,3,2,1,0:T(8,128)(2,1)} %get-tuple-element.7.node_hbm, bf16[12,16,128]{2,1,0:T(8,128)(2,1)} %get-tuple-element.8.w1_hbm), custom_call_target="tpu_custom_call" | custom-call | tf_op jit(solution)/shard_map/pallas_call | solution.py:556

commit v3 on v2

v3 whole, which is shorter than its diff:
```python
import functools

import jax
import jax.numpy as jnp
from jax import lax
from jax.experimental import pallas as pl
from jax.experimental.pallas import tpu as pltpu
from jax.sharding import PartitionSpec as P

F32 = jnp.float32
BF16 = jnp.bfloat16
SLOTS = 8


def dot(a, b, ca=1, cb=0):
    return lax.dot_general(a, b, (((ca,), (cb,)), ((), ())), preferred_element_type=F32)


def iota(shape, dim):
    return lax.broadcasted_iota(jnp.int32, shape, dim)


def each(n, fn):
    group = 7 if n > 8 and (n - 1) % 7 == 0 else 1

    def step(i, carry):
        for j in range(group):
            fn(i * group + j + 1)
        return carry

    lax.fori_loop(0, (n - 1) // group, step, 0)


def push(src, dst, send_sem, recv_sem, device):
    return pltpu.make_async_remote_copy(
        src_ref=src,
        dst_ref=dst,
        send_sem=send_sem,
        recv_sem=recv_sem,
        device_id=device,
        device_id_type=pl.DeviceIdType.MESH,
    )


def kernel(
    ny, nx, ng,
    ids_hbm, users_hbm, lg_hbm, b_hbm, wout_hbm, table_hbm, win_hbm,
    ug_out, anode, aw,
    ids_ref, users_ref, lg_ref, b_ref, wout_ref, table, win,
    place, place_t, select_t, base, pgs, weights, spread, ug,
    src1, out1, src2, out2, src3, out3,
    ucol, ssend, srecv, qusend, qurecv, psend, pswap, pdir, pin,
    znode, rrel, rdir, hsum, bnode, afar, zw, rw, bw,
    load_sem, own_sem, d_send, d_recv, y_send, y_recv, c_send, c_recv, s_send, s_recv,
    u_send, u_recv, p_send, p_recv, z_send, z_recv, zn_send, zn_recv,
):
    rows, per_row = ids_ref.shape
    nodes = table.shape[0]
    width = table.shape[1]
    hid = win.shape[1]
    du = users_ref.shape[1]
    pairs = rows * per_row
    padded = place.shape[0]
    slots = place.shape[1]
    shards = ny * nx
    hb = hid // shards
    band = nx * hb

    g = lax.axis_index("grp")
    me = lax.axis_index("sub")
    y = me // nx
    x = me % nx
    c = x % 2
    xch = x // 2
    nxc = nx // 2
    chips = ny * nxc
    chip = me // 2
    q = y * 2 + c

    loads = [
        pltpu.make_async_copy(src, dst, load_sem.at[n])
        for n, (src, dst) in enumerate(
            [
                (ids_hbm, ids_ref),
                (users_hbm, users_ref),
                (win_hbm, win),
                (table_hbm, table),
                (b_hbm, b_ref),
                (wout_hbm, wout_ref),
                (lg_hbm, lg_ref),
            ]
        )
    ]
    for load in loads:
        load.start()
    load_ids, load_users, load_win, load_table, *load_small = loads

    def y_peer(d):
        return {"sub": ((y + d) % ny) * nx + x}

    partner = {"sub": chip * 2 + 1 - c}

    def sub_peer(d):
        return {"sub": (me + d) % shards}

    def z_peer(d):
        return {"grp": (g + d) % ng}

    barrier = pltpu.get_barrier_semaphore()

    def greet(peer):
        def go(d):
            pl.semaphore_signal(
                barrier, inc=1, device_id=peer(d), device_id_type=pl.DeviceIdType.MESH
            )

        return go

    each(shards, greet(sub_peer))
    each(ng, greet(z_peer))

    lanes = 128
    half = lanes // 2
    before = (iota((padded, padded), 0) > iota((padded, padded), 1)).astype(F32).astype(BF16)
    slot_row = iota((slots, lanes), 0) % SLOTS
    slot_col = iota((slots, lanes), 1)
    weight = jnp.where(slot_col == slot_row, 32.0, 0.0)
    weights[...] = weight + jnp.where(slot_col == slot_row + half, 1.0, 0.0)
    spread[...] = (
        (iota((slots, shards), 0) // SLOTS == iota((slots, shards), 1)).astype(F32).astype(BF16)
    )
    load_ids.wait()
    ids = ids_ref[...]
    cols = jnp.concatenate(
        [jnp.broadcast_to(ids[:, k : k + 1], (rows, lanes)) for k in range(per_row)]
        + [jnp.full((padded - pairs, lanes), -1, jnp.int32)],
        axis=0,
    )
    shift = nodes.bit_length() - 1
    owner = lax.shift_right_arithmetic(cols, jnp.int32(shift))
    local = cols & (nodes - 1)
    lane = iota((padded, lanes), 1)
    hit = (owner == lane).astype(F32)
    hit_low = hit.astype(BF16)
    rank = jnp.sum(dot(before, hit_low) * hit, axis=1, keepdims=True)
    slot_lane = rank.astype(jnp.int32)
    high, low = lax.shift_right_arithmetic(local, jnp.int32(5)) + 1, local & 31
    asked = jnp.where(lane == slot_lane, high, jnp.where(lane == slot_lane + half, low, 0))
    request = dot(hit_low, asked.astype(F32).astype(BF16), 0, 0)
    src1[...] = request[0:shards].reshape(shards, 1, lanes)

    pl.semaphore_wait(barrier, (shards - 1) + (ng - 1))

    def y_stage(num, src, dst):
        return lambda d: push(
            src((y + d) % ny), dst.at[y], y_send.at[num, d], y_recv.at[num, d], y_peer(d)
        )

    def y_arrival(num, src, dst):
        return lambda d: push(
            src(y), dst.at[(y + ny - d) % ny], y_send.at[num, d], y_recv.at[num, d], y_peer(d)
        )

    def z_stage(num, src, dst):
        return lambda d: push(
            src((g + d) % ng), dst.at[g], z_send.at[num, d], z_recv.at[num, d], z_peer(d)
        )

    def z_arrival(num, src, dst):
        return lambda d: push(
            src(g), dst.at[(g + ng - d) % ng], z_send.at[num, d], z_recv.at[num, d], z_peer(d)
        )

    def d_stage(num, src, dst):
        return lambda d: push(
            src.at[(me + d) % shards], dst.at[me], d_send.at[num], d_recv.at[num], sub_peer(d)
        )

    def d_all(num, src, dst):
        rest = pl.ds(0, shards - 1)
        return push(src.at[rest], dst.at[rest], d_send.at[num], d_recv.at[num], sub_peer(1))

    def go(n, make):
        each(n, lambda d: make(d).start())

    def come(n, make):
        each(n, lambda d: make(d).wait_recv())

    def gone(n, make):
        each(n, lambda d: make(d).wait_send())

    def by_lead(ref):
        return lambda t: ref.at[t]

    def whole(ref):
        return lambda t: ref

    go(shards, d_stage(0, src1, out1))
    out1[me] = src1[me]

    load_users.wait()
    go(ny, y_stage(0, whole(users_ref), ucol.at[:, c]))
    ucol[y, c] = users_ref[...]
    load_win.wait()
    for load in load_small:
        load.wait()
    base[...] = dot(users_ref[...], win[0:du, :]) + b_ref[...]
    load_table.wait()
    d_all(0, src1, out1).wait_recv()

    wanted = dot(spread[...], out1[...].reshape(shards, lanes).astype(BF16))
    place_of = jnp.sum(wanted * weights[...], axis=1, keepdims=True) - 32.0
    select = (iota((slots, nodes), 1).astype(F32) == place_of).astype(F32)
    fetched = dot(select.astype(BF16), table[...])
    src2[...] = fetched.reshape(shards, SLOTS, width).astype(BF16)
    go(shards, d_stage(1, src2, out2))
    out2[me] = src2[me]
    place_row = jnp.broadcast_to(place_of, (slots, lanes)).T[0:1]
    select_t[...] = (iota((nodes, slots), 0).astype(F32) == place_row).astype(F32).astype(BF16)
    code = owner.astype(F32) * float(SLOTS) + rank
    chosen = (iota((padded, slots), 1).astype(F32) == code[:, 0:1]).astype(F32)
    place[...] = chosen.astype(BF16)
    code_row = code.T[0:1]
    place_t[...] = (iota((slots, padded), 0).astype(F32) == code_row).astype(F32).astype(BF16)
    come(ny, y_arrival(0, whole(users_ref), ucol.at[:, c]))
    swap_users = push(ucol.at[:, c], ucol.at[:, c], c_send.at[0], c_recv.at[0], partner)
    swap_users.start()
    d_all(1, src2, out2).wait_recv()

    returned = out2[...].astype(F32).reshape(slots, width).astype(BF16)
    pn = dot(place[0:pairs, :], returned).astype(BF16)
    grad_col = jnp.concatenate([lg_ref[:, k : k + 1] for k in range(per_row)], axis=0)
    step = min(hid, 512)
    sums = []
    for left in range(0, hid, step):
        cut = slice(left, left + step)
        part = dot(pn, win[du:, cut]).reshape(per_row, rows, step)
        pre = (part + base[:, cut][None]).reshape(pairs, step)
        squash = jax.nn.sigmoid(pre)
        pre_grad = (
            (grad_col * wout_ref[:, cut]) * (squash * (1.0 + pre * (1.0 - squash)))
        ).astype(BF16)
        pgs[:, cut] = pre_grad
        sums.append(jnp.sum(pre_grad.astype(F32).reshape(per_row, rows, step), axis=0))
    in_grad = dot(pgs[...], win[du:, :], 1, 1).astype(BF16)
    back = dot(place_t[:, 0:pairs], in_grad)

    src3[...] = back.reshape(shards, SLOTS, width).astype(BF16)
    go(shards, d_stage(2, src3, out3))
    out3[me] = src3[me]

    row_sum = jnp.concatenate(sums, axis=1)
    bh = band // 2
    for i in range(2 * ny):
        ssend[i] = row_sum[:, i * bh : (i + 1) * bh].astype(BF16)

    def s_stage(d):
        t = (q + d) % (2 * ny)
        return push(
            ssend.at[t], srecv.at[q], s_send.at[d], s_recv.at[d],
            {"sub": (t // 2) * nx + xch * 2 + t % 2},
        )

    def s_arrival(d):
        return push(
            ssend.at[q], srecv.at[(q + 2 * ny - d) % (2 * ny)], s_send.at[d], s_recv.at[d], partner
        )

    go(2 * ny, s_stage)
    srecv[q] = ssend[q]

    pn_t = pn.astype(F32).T.astype(BF16)
    parts = 2 if ny % 2 == 0 else 1
    bands = ny // parts

    def p_swap(h):
        part = slice(h * bands, (h + 1) * bands)
        return push(
            psend.at[1 - c, part], pswap.at[part], c_send.at[1 + h], c_recv.at[1 + h], partner
        )

    for h in range(parts):
        for j in range(h * bands, (h + 1) * bands):
            prod = dot(pn_t, pgs[:, j * band : (j + 1) * band]).T.astype(BF16)
            for i in range(nx):
                psend[i % 2, j, i // 2] = prod[i * hb : (i + 1) * hb]
        p_swap(h).start()
    for h in range(parts):
        p_swap(h).wait_recv()
        part = slice(h * bands, (h + 1) * bands)
        mine = psend[c, part].astype(F32) + pswap[part].astype(F32)
        pdir[h * bands * nxc : (h + 1) * bands * nxc] = mine.reshape(
            bands * nxc, hb, width
        ).astype(BF16)

    def p_stage(d):
        t = (chip + d) % chips
        return push(
            pdir.at[t], pin.at[chip], p_send.at[d], p_recv.at[d], {"sub": t * 2 + c}
        )

    def p_arrival(d):
        return push(
            pdir.at[chip], pin.at[(chip + chips - d) % chips], p_send.at[d], p_recv.at[d], partner
        )

    go(chips, p_stage)
    pin[chip] = pdir[chip]

    swap_users.wait_recv()
    come(2 * ny, s_arrival)
    user_cols = dot(
        srecv[...].reshape(2 * ny * rows, bh), ucol[...].reshape(2 * ny * rows, du), 0, 0
    ).astype(BF16)
    for m in range(nxc):
        qusend[m] = user_cols[m * hb : (m + 1) * hb]

    def u_stage(m):
        at = (xch + m) % nxc
        return push(
            qusend.at[at], qurecv.at[xch], u_send.at[at], u_recv.at[xch],
            {"sub": y * nx + c * nxc + at},
        )

    def u_arrival(i):
        return push(qusend.at[0], qurecv.at[i], u_send.at[0], u_recv.at[i], partner)

    for m in range(nxc):
        at = (xch + m) % nxc

        @pl.when(c * nxc + at != x)
        def _():
            u_stage(m).start()

        @pl.when(c * nxc + at == x)
        def _():
            qurecv[xch] = qusend[at]

    d_all(2, src3, out3).wait_recv()
    arrived = out3[...].astype(F32).reshape(slots, width).astype(BF16)
    node_part = dot(select_t[...], arrived).reshape(nodes // 8, 8, width).astype(BF16)
    zu = znode.shape[1]
    units = nodes // 8
    for o in range(ng):
        lo, hi = min(o * zu, units), min((o + 1) * zu, units)
        if hi > lo:
            znode[o, 0 : hi - lo] = node_part[lo:hi]
        if hi - lo < zu:
            znode[o, hi - lo :] = jnp.zeros((zu - (hi - lo), 8, width), BF16)
    far = ng // 2
    relay = far // 2
    near_by = [(i, k) for k in range(relay - 1, 0, -1) for i in (0, 1)]
    beyond = [(i, k) for k in range(far - 1, relay, -1) for i in (0, 1)]

    def off(i, k):
        return (g + k * (1 - 2 * i) + ng) % ng

    def z_push(phase, i, k, src, dst, hop):
        return push(
            src, dst, zn_send.at[phase, i, k], zn_recv.at[phase, i, k], {"grp": off(i, hop)}
        )

    def rs_to_relay(i, k):
        return z_push(0, i, k, znode.at[off(i, -k)], rrel.at[i, k], relay - k)

    def rs_direct(i, k):
        return z_push(0, i, k, znode.at[off(i, -k)], rdir.at[i, k], -k)

    def rs_relay(i):
        return z_push(0, i, relay, hsum.at[i], rdir.at[i, relay], -relay)

    def ag_direct(i, k):
        return z_push(1, i, k, bnode, anode.at[g], k)

    def ag_to_relay(i):
        return z_push(1, i, relay, bnode, afar.at[i], relay)

    def ag_from_relay(i, k):
        return z_push(1, i, k, afar.at[i], anode.at[off(i, -relay)], k - relay)

    def ag_arrival(i, k):
        return z_push(1, i, k, bnode, anode.at[off(i, -k)], k)

    rs_to_relay(c, far).start()
    for i, k in beyond:
        rs_to_relay(i, k).start()
    for i, k in near_by:
        rs_direct(i, k).start()

    for turn in (1, 0):
        i = (c + turn) % 2
        part = znode[off(i, -relay)].astype(F32)
        for k in range(relay + 1, far + (1 - turn)):
            rs_to_relay(i, k).wait_recv()
            part = part + rrel[i, k].astype(F32)
        hsum[i] = part.astype(BF16)
        rs_relay(i).start()

    come(chips, p_arrival)
    for m in range(nxc):

        @pl.when(m * 2 + x // nxc != x)
        def _():
            u_arrival(m).wait_recv()

    user_block = qurecv[0].astype(F32)
    for j in range(1, nxc):
        user_block = user_block + qurecv[j].astype(F32)
    node_block = pin[0].astype(F32)
    for j in range(1, chips):
        node_block = node_block + pin[j].astype(F32)
    block = jnp.concatenate([user_block, node_block], axis=1).astype(BF16)
    tiles = w1_tiles(hb, du + width)
    per = zw.shape[1] // 16
    for n in range(ng * per):
        at = (n // per, slice((n % per) * 16, (n % per) * 16 + 16))
        if n < len(tiles):
            down, over = tiles[n]
            zw[at] = block[down * 16 : down * 16 + 16, over * lanes : (over + 1) * lanes]
        else:
            zw[at] = jnp.zeros((16, lanes), BF16)
    go(ng, z_stage(0, by_lead(zw), rw))
    rw[g] = zw[g]

    mine = znode[g].astype(F32)
    for i, k in [(i, k) for k in range(1, relay + 1) for i in (0, 1)]:
        rs_direct(i, k).wait_recv()
        mine = mine + rdir[i, k].astype(F32)
    bnode[...] = mine.astype(BF16)
    for i in (0, 1):
        ag_to_relay(i).start()
    for i, k in near_by:
        ag_direct(i, k).start()
    keep_own = pltpu.make_async_copy(bnode, anode.at[g], own_sem.at[0])
    keep_own.start()

    come(ng, z_arrival(0, by_lead(zw), rw))
    tile_sum = rw[0].astype(F32)
    for j in range(1, ng):
        tile_sum = tile_sum + rw[j].astype(F32)
    bw[...] = tile_sum.astype(BF16)
    go(ng, z_stage(1, whole(bw), aw))
    keep_w = pltpu.make_async_copy(bw, aw.at[g], own_sem.at[1])
    keep_w.start()

    keep_far = []
    for turn in (0, 1):
        i = (c + turn) % 2
        ag_to_relay(i).wait_recv()
        for k in range(far - turn, relay, -1):
            ag_from_relay(i, k).start()
        copy = pltpu.make_async_copy(afar.at[i], anode.at[off(i, -relay)], own_sem.at[2 + turn])
        copy.start()
        keep_far.append(copy)

    ug[...] = dot(row_sum.astype(BF16), win[0:du, :], 1, 1)
    keep_ug = pltpu.make_async_copy(ug, ug_out, load_sem.at[0])
    keep_ug.start()
    for i, k in near_by[::-1] + beyond[::-1]:
        ag_arrival(i, k).wait_recv()
    ag_arrival(c, far).wait_recv()
    come(ng, z_arrival(1, whole(bw), aw))
    keep_ug.wait()
    keep_own.wait()
    keep_w.wait()
    for copy in keep_far:
        copy.wait()

    rs_to_relay(c, far).wait_send()
    ag_from_relay(c, far).wait_send()
    for i, k in beyond:
        rs_to_relay(i, k).wait_send()
        ag_from_relay(i, k).wait_send()
    for i, k in near_by:
        rs_direct(i, k).wait_send()
        ag_direct(i, k).wait_send()
    for i in (0, 1):
        rs_relay(i).wait_send()
        ag_to_relay(i).wait_send()
    d_all(0, src1, out1).wait_send()
    d_all(1, src2, out2).wait_send()
    d_all(2, src3, out3).wait_send()
    gone(ny, y_stage(0, whole(users_ref), ucol.at[:, c]))
    swap_users.wait_send()
    gone(2 * ny, s_stage)
    for h in range(parts):
        p_swap(h).wait_send()
    gone(chips, p_stage)
    for m in range(nxc):

        @pl.when(c * nxc + (xch + m) % nxc != x)
        def _():
            u_stage(m).wait_send()

    gone(ng, z_stage(0, by_lead(zw), rw))
    gone(ng, z_stage(1, whole(bw), aw))


def finish(
    devices, ug_hbm, node_hbm, w1_hbm, ug_out, node_out, w1_out,
    ug, node_in, w1_in, node, w1, in_sem, out_sem,
):
    ng, zu, _, width = node_in.shape
    units, (hb, din) = node.shape[0] // 8, w1.shape
    loads = [
        pltpu.make_async_copy(src, dst, in_sem.at[n])
        for n, (src, dst) in enumerate([(node_hbm, node_in), (w1_hbm, w1_in), (ug_hbm, ug)])
    ]
    stores = [
        pltpu.make_async_copy(src, dst, out_sem.at[n])
        for n, (src, dst) in enumerate([(node, node_out), (w1, w1_out), (ug, ug_out)])
    ]
    for load in loads:
        load.start()
    loads[0].wait()
    for o in range(ng):
        lo, hi = min(o * zu, units), min((o + 1) * zu, units)
        if hi > lo:
            part = node_in[o, 0 : hi - lo].astype(F32)
            node[lo * 8 : hi * 8] = part.reshape((hi - lo) * 8, width)
    stores[0].start()
    loads[2].wait()
    stores[2].start()
    loads[1].wait()
    per = w1_in.shape[1] // 16
    for n, (a, c) in enumerate(w1_tiles(hb, din)):
        part = w1_in[n // per, (n % per) * 16 : (n % per) * 16 + 16].astype(F32)
        w1[a * 16 : a * 16 + 16, c * 128 : (c + 1) * 128] = part / devices
    stores[1].start()
    for store in stores:
        store.wait()


def w1_tiles(hb, din):
    return [(a, c) for a in range(hb // 16) for c in range(din // 128)]


def local(ng, shards, users, node_ids, node_table, w_in, b_in, w_out, logit_grad):
    nx = 8 if shards > 8 and shards % 8 == 0 else 2
    ny = shards // nx
    rows, per_row = node_ids.shape
    du = users.shape[1]
    nodes, width = node_table.shape
    din, hid = w_in.shape
    pairs = rows * per_row
    padded = -(-pairs // 128) * 128
    slots = shards * SLOTS
    hb = hid // shards
    zu = -(-nodes // (ng * 8))
    nxc = nx // 2
    far = ng // 2 + 1
    block = (zu, 8, width)
    zt = -(-len(w1_tiles(hb, din)) // ng) * 16
    hbm = pl.BlockSpec(memory_space=pltpu.HBM)

    parts = pl.pallas_call(
        functools.partial(kernel, ny, nx, ng),
        out_shape=(
            jax.ShapeDtypeStruct((rows, du), F32),
            jax.ShapeDtypeStruct((ng, *block), BF16),
            jax.ShapeDtypeStruct((ng, zt, 128), BF16),
        ),
        in_specs=[hbm] * 7,
        out_specs=(hbm, hbm, hbm),
        scratch_shapes=[
            pltpu.VMEM((rows, per_row), jnp.int32),
            pltpu.VMEM((rows, du), BF16),
            pltpu.VMEM((rows, per_row), F32),
            pltpu.VMEM((1, hid), F32),
            pltpu.VMEM((1, hid), F32),
            pltpu.VMEM((nodes, width), BF16),
            pltpu.VMEM((din, hid), BF16),
            pltpu.VMEM((padded, slots), BF16),
            pltpu.VMEM((slots, padded), BF16),
            pltpu.VMEM((nodes, slots), BF16),
            pltpu.VMEM((rows, hid), F32),
            pltpu.VMEM((pairs, hid), BF16),
            pltpu.VMEM((slots, 128), F32),
            pltpu.VMEM((slots, shards), BF16),
            pltpu.VMEM((rows, du), F32),
            *[pltpu.VMEM((shards, 1, 128), F32)] * 2,
            *[pltpu.VMEM((shards, SLOTS, width), BF16)] * 4,
            pltpu.VMEM((ny, 2, rows, du), BF16),
            *[pltpu.VMEM((2 * ny, rows, nxc * hb), BF16)] * 2,
            *[pltpu.VMEM((nxc, hb, du), BF16)] * 2,
            pltpu.VMEM((2, ny, nxc, hb, width), BF16),
            pltpu.VMEM((ny, nxc, hb, width), BF16),
            *[pltpu.VMEM((ny * nxc, hb, width), BF16)] * 2,
            pltpu.VMEM((ng, *block), BF16),
            *[pltpu.VMEM((2, far, *block), BF16)] * 2,
            pltpu.VMEM((2, *block), BF16),
            pltpu.VMEM(block, BF16),
            pltpu.VMEM((2, *block), BF16),
            pltpu.VMEM((ng, zt, 128), BF16),
            pltpu.VMEM((ng, zt, 128), BF16),
            pltpu.VMEM((zt, 128), BF16),
            pltpu.SemaphoreType.DMA((7,)),
            pltpu.SemaphoreType.DMA((4,)),
            *[pltpu.SemaphoreType.DMA((3,))] * 2,
            *[pltpu.SemaphoreType.DMA((1, ny))] * 2,
            *[pltpu.SemaphoreType.DMA((3,))] * 2,
            *[pltpu.SemaphoreType.DMA((2 * ny,))] * 2,
            *[pltpu.SemaphoreType.DMA((nxc,))] * 2,
            *[pltpu.SemaphoreType.DMA((ny * nxc,))] * 2,
            *[pltpu.SemaphoreType.DMA((2, ng))] * 2,
            *[pltpu.SemaphoreType.DMA((2, 2, far))] * 2,
        ],
        compiler_params=pltpu.CompilerParams(
            collective_id=0, has_side_effects=True, vmem_limit_bytes=60 * 2**20
        ),
    )(
        node_ids, users, logit_grad, b_in.reshape(1, hid), w_out.reshape(1, hid),
        node_table, w_in,
    )
    return pl.pallas_call(
        functools.partial(finish, float(shards * ng)),
        out_shape=(
            jax.ShapeDtypeStruct((rows, du), F32),
            jax.ShapeDtypeStruct((nodes, width), F32),
            jax.ShapeDtypeStruct((hb, din), F32),
        ),
        in_specs=[hbm] * 3,
        out_specs=(hbm, hbm, hbm),
        scratch_shapes=[
            pltpu.VMEM((rows, du), F32),
            pltpu.VMEM((ng, *block), BF16),
            pltpu.VMEM((ng, zt, 128), BF16),
            pltpu.VMEM((nodes, width), F32),
            pltpu.VMEM((hb, din), F32),
            pltpu.SemaphoreType.DMA((3,)),
            pltpu.SemaphoreType.DMA((3,)),
        ],
        compiler_params=pltpu.CompilerParams(vmem_limit_bytes=60 * 2**20),
    )(*parts)


def solution(mesh):
    ng, shards = mesh.shape["grp"], mesh.shape["sub"]
    return jax.shard_map(
        functools.partial(local, ng, shards),
        mesh=mesh,
        in_specs=(
            P(("grp", "sub"), None),
            P(("grp", "sub"), None),
            P("sub", None),
            P(),
            P(),
            P(),
            P(("grp", "sub"), None),
        ),
        out_specs=(P(("grp", "sub"), None), P("sub", None), P("sub", None)),
        check_vma=False,
    )
```

time: 72.9 us -> 69.9 us (0.959)
  the two profiles are of different devices: /device:TPU:2 before, /device:TPU:56 now
where the time goes in v3:
time: 69.9 us; the launch traced here: 69.8 us
  Pallas kernels  69.1 us (99%)
    pallas_call x1, Pallas kernels, local(): pl.pallas_call(functools.partial(kernel, ny, nx, ng), out_shape=(jax.Shap...  67.3 us
    pallas_call x1, Pallas kernels, local(): pl.pallas_call(functools.partial(finish, float(shards * ng)), out_shape=(...  1.86 us

profile of v3, /device:TPU:56, one launch (start us, length us, event | category | flops | bytes accessed | tf_op | source)
XLA Modules:
  0.0 69.8 jit_solution(2413151791293464527)
XLA Ops:
  0.6 67.3 %shard_map.94 = (f32[16,512]{1,0:T(8,128)}, bf16[12,11,8,128]{3,2,1,0:T(8,128)(2,1)}, bf16[12,16,128]{2,1,0:T(8,128)(2,1)}) custom-call(s32[16,14]{1,0:T(8,128)} %ids_hbm.1, bf16[16,512]{1,0:T(8,128)(2,1)} %users_hbm.1, f32[16,14]{1,0:T(8,128)} %lg_hbm.1, f32[1,2048]{1,0:T(1,128)} %bitcast.2, f32[1,2048]{1,0:T(1,128)} %bitcast.3, ...), custom_call_target="tpu_custom_call" | custom-call | tf_op jit(solution)/shard_map/pallas_call | solution.py:556
  67.9 1.9 %shard_map.95 = (f32[16,512]{1,0:T(8,128)}, f32[1024,128]{1,0:T(8,128)}, f32[32,640]{1,0:T(8,128)}) custom-call(f32[16,512]{1,0:T(8,128)} %get-tuple-element.6.ug_hbm, bf16[12,11,8,128]{3,2,1,0:T(8,128)(2,1)} %get-tuple-element.7.node_hbm, bf16[12,16,128]{2,1,0:T(8,128)(2,1)} %get-tuple-element.8.w1_hbm), custom_call_target="tpu_custom_call" | custom-call | tf_op jit(solution)/shard_map/pallas_call | solution.py:615

commit v4 on v3

--- a/solution.py
+++ b/solution.py
@@ -171,10 +171,19 @@
             src(g), dst.at[(g + ng - d) % ng], z_send.at[num, d], z_recv.at[num, d], z_peer(d)
         )
 
-    def d_stage(num, src, dst):
-        return lambda d: push(
-            src.at[(me + d) % shards], dst.at[me], d_send.at[num], d_recv.at[num], sub_peer(d)
-        )
+    def send_all(num, src, dst):
+        def one(t):
+            push(src.at[t], dst.at[me], d_send.at[num], d_recv.at[num], {"sub": t}).start()
+
+        def row(i, carry):
+            dy = ny // 2 + ((i + 1) // 2) * (1 - 2 * (i % 2))
+            for dx in range(nx):
+                one(((y + dy) % ny) * nx + (x + dx) % nx)
+            return carry
+
+        lax.fori_loop(0, ny - 1, row, 0)
+        for dx in range(1, nx):
+            one(y * nx + (x + dx) % nx)
 
     def d_all(num, src, dst):
         rest = pl.ds(0, shards - 1)
@@ -195,11 +204,10 @@
     def whole(ref):
         return lambda t: ref
 
-    go(shards, d_stage(0, src1, out1))
+    send_all(0, src1, out1)
     out1[me] = src1[me]
 
     load_users.wait()
-    go(ny, y_stage(0, whole(users_ref), ucol.at[:, c]))
     ucol[y, c] = users_ref[...]
     load_win.wait()
     for load in load_small:
@@ -213,7 +221,7 @@
     select = (iota((slots, nodes), 1).astype(F32) == place_of).astype(F32)
     fetched = dot(select.astype(BF16), table[...])
     src2[...] = fetched.reshape(shards, SLOTS, width).astype(BF16)
-    go(shards, d_stage(1, src2, out2))
+    send_all(1, src2, out2)
     out2[me] = src2[me]
     place_row = jnp.broadcast_to(place_of, (slots, lanes)).T[0:1]
     select_t[...] = (iota((nodes, slots), 0).astype(F32) == place_row).astype(F32).astype(BF16)
@@ -222,9 +230,7 @@
     place[...] = chosen.astype(BF16)
     code_row = code.T[0:1]
     place_t[...] = (iota((slots, padded), 0).astype(F32) == code_row).astype(F32).astype(BF16)
-    come(ny, y_arrival(0, whole(users_ref), ucol.at[:, c]))
-    swap_users = push(ucol.at[:, c], ucol.at[:, c], c_send.at[0], c_recv.at[0], partner)
-    swap_users.start()
+    go(ny, y_stage(0, whole(users_ref), ucol.at[:, c]))
     d_all(1, src2, out2).wait_recv()
 
     returned = out2[...].astype(F32).reshape(slots, width).astype(BF16)
@@ -246,9 +252,12 @@
     back = dot(place_t[:, 0:pairs], in_grad)
 
     src3[...] = back.reshape(shards, SLOTS, width).astype(BF16)
-    go(shards, d_stage(2, src3, out3))
+    send_all(2, src3, out3)
     out3[me] = src3[me]
 
+    come(ny, y_arrival(0, whole(users_ref), ucol.at[:, c]))
+    swap_users = push(ucol.at[:, c], ucol.at[:, c], c_send.at[0], c_recv.at[0], partner)
+    swap_users.start()
     row_sum = jnp.concatenate(sums, axis=1)
     bh = band // 2
     for i in range(2 * ny):
@@ -295,14 +304,11 @@
 
     def p_stage(d):
         t = (chip + d) % chips
-        return push(
-            pdir.at[t], pin.at[chip], p_send.at[d], p_recv.at[d], {"sub": t * 2 + c}
-        )
-
-    def p_arrival(d):
-        return push(
-            pdir.at[chip], pin.at[(chip + chips - d) % chips], p_send.at[d], p_recv.at[d], partner
-        )
+        return push(pdir.at[t], pin.at[chip], p_send, p_recv, {"sub": t * 2 + c})
+
+    def p_all():
+        rest = pl.ds(0, chips - 1)
+        return push(pdir.at[rest], pin.at[rest], p_send, p_recv, partner)
 
     go(chips, p_stage)
     pin[chip] = pdir[chip]
@@ -387,16 +393,7 @@
     for i, k in near_by:
         rs_direct(i, k).start()
 
-    for turn in (1, 0):
-        i = (c + turn) % 2
-        part = znode[off(i, -relay)].astype(F32)
-        for k in range(relay + 1, far + (1 - turn)):
-            rs_to_relay(i, k).wait_recv()
-            part = part + rrel[i, k].astype(F32)
-        hsum[i] = part.astype(BF16)
-        rs_relay(i).start()
-
-    come(chips, p_arrival)
+    p_all().wait_recv()
     for m in range(nxc):
 
         @pl.when(m * 2 + x // nxc != x)
@@ -421,6 +418,15 @@
             zw[at] = jnp.zeros((16, lanes), BF16)
     go(ng, z_stage(0, by_lead(zw), rw))
     rw[g] = zw[g]
+
+    for turn in (1, 0):
+        i = (c + turn) % 2
+        part = znode[off(i, -relay)].astype(F32)
+        for k in range(relay + 1, far + (1 - turn)):
+            rs_to_relay(i, k).wait_recv()
+            part = part + rrel[i, k].astype(F32)
+        hsum[i] = part.astype(BF16)
+        rs_relay(i).start()
 
     mine = znode[g].astype(F32)
     for i, k in [(i, k) for k in range(1, relay + 1) for i in (0, 1)]:
@@ -485,7 +491,7 @@
     gone(2 * ny, s_stage)
     for h in range(parts):
         p_swap(h).wait_send()
-    gone(chips, p_stage)
+    p_all().wait_send()
     for m in range(nxc):
 
         @pl.when(c * nxc + (xch + m) % nxc != x)
@@ -601,7 +607,7 @@
             *[pltpu.SemaphoreType.DMA((3,))] * 2,
             *[pltpu.SemaphoreType.DMA((2 * ny,))] * 2,
             *[pltpu.SemaphoreType.DMA((nxc,))] * 2,
-            *[pltpu.SemaphoreType.DMA((ny * nxc,))] * 2,
+            *[pltpu.SemaphoreType.DMA] * 2,
             *[pltpu.SemaphoreType.DMA((2, ng))] * 2,
             *[pltpu.SemaphoreType.DMA((2, 2, far))] * 2,
         ],

time: 69.9 us -> 68.5 us (0.980); the launches traced: 69.8 us -> 67.3 us
  Pallas kernels: 69.1 us -> 66.6 us
    pallas_call x1, Pallas kernels: 67.3 us -> 64.8 us  [local(): pl.pallas_call(functools.partial(kernel, ny, nx, ng), out_shape=(jax.Shap...]
where the time goes in v4:
time: 68.5 us; the launch traced here: 67.3 us
  Pallas kernels  66.6 us (97%)
    pallas_call x1, Pallas kernels, local(): pl.pallas_call(functools.partial(kernel, ny, nx, ng), out_shape=(jax.Shap...  64.8 us
    pallas_call x1, Pallas kernels, local(): pl.pallas_call(functools.partial(finish, float(shards * ng)), out_shape=(...  1.86 us

profile of v4, /device:TPU:56, one launch (start us, length us, event | category | flops | bytes accessed | tf_op | source)
XLA Modules:
  0.0 67.3 jit_solution(15822755977718890199)
XLA Ops:
  0.6 64.8 %shard_map.94 = (f32[16,512]{1,0:T(8,128)}, bf16[12,11,8,128]{3,2,1,0:T(8,128)(2,1)}, bf16[12,16,128]{2,1,0:T(8,128)(2,1)}) custom-call(s32[16,14]{1,0:T(8,128)} %ids_hbm.1, bf16[16,512]{1,0:T(8,128)(2,1)} %users_hbm.1, f32[16,14]{1,0:T(8,128)} %lg_hbm.1, f32[1,2048]{1,0:T(1,128)} %bitcast.2, f32[1,2048]{1,0:T(1,128)} %bitcast.3, ...), custom_call_target="tpu_custom_call" | custom-call | tf_op jit(solution)/shard_map/pallas_call | solution.py:562
  65.4 1.9 %shard_map.95 = (f32[16,512]{1,0:T(8,128)}, f32[1024,128]{1,0:T(8,128)}, f32[32,640]{1,0:T(8,128)}) custom-call(f32[16,512]{1,0:T(8,128)} %get-tuple-element.6.ug_hbm, bf16[12,11,8,128]{3,2,1,0:T(8,128)(2,1)} %get-tuple-element.7.node_hbm, bf16[12,16,128]{2,1,0:T(8,128)(2,1)} %get-tuple-element.8.w1_hbm), custom_call_target="tpu_custom_call" | custom-call | tf_op jit(solution)/shard_map/pallas_call | solution.py:621
